TPU v7x, 32 devices: a whole 2x2x4 slice. The times are simulated.
32 devices in a mesh: row: 4 (over y, x), col: 8 (over z, core).
Axes of the slice: x: 2, y: 2, z: 4, core: 2. Of those that a mesh axis runs over, the one named last changes fastest.
Arguments:
- latent: bfloat16 [16, 131072], P(None, ('row', 'col')), may hold values from -200 to 200, as said below
- in_weight: bfloat16 [3, 3, 16, 512], replicated, may hold values from -0.5 to 0.5
- in_bias: float32 [512], replicated, may hold values from -3 to 3
- norm_gain: float32 [512], replicated, may hold values from 0.25 to 1.75
- norm_shift: float32 [512], replicated, may hold values from -3 to 3
- mid_weight: bfloat16 [512, 3, 3, 512], replicated, may hold values from -0.09375 to 0.09375
- mid_bias: float32 [512], replicated, may hold values from -3 to 3
Outputs:
- features: bfloat16 [256, 512, 512], P('row', 'col')
Inputs may be any that keep to these rules, and one draw needn't show every extreme that they name: real-valued latent entries.
All inputs are finite; a program needn't handle non-finite values.
Results may differ from a plain program's by a relative error of at most 0.0095.
Values may be sent and summed in bfloat16 or wider, within the bound.
A program may use at most 192 MiB of HBM per device.

v0:
```python
import functools

import jax
import jax.numpy as jnp
from jax import lax
from jax.experimental import pallas as pl
from jax.experimental.pallas import tpu as pltpu
from jax.sharding import PartitionSpec as P

GROUPS = 32
TILE_W = 64
EPSILON = 1e-06
LANES = 128
MESH = pl.DeviceIdType.MESH
COLS_PAD = 80
ROWS_STEP = 4


def front_kernel(
    n_row, n_col, lat_ref, w_ref, bias_ref, gain_ref, shift_ref,
    fo_ref, ss_ref,
    send, x_ref, xs_ref, part, slot_col, part_row, slot_row,
    send_sem, recv_sem, halo_send, halo_recv, s1_send, s1_recv, s2_send, s2_recv,
):
    row, col = lax.axis_index("row"), lax.axis_index("col")
    c_lat = lat_ref.shape[0]
    breadth = TILE_W * n_col
    rp = lat_ref.shape[1] // breadth
    tile_h = rp * n_col

    barrier = pltpu.get_barrier_semaphore()
    for k in range(1, n_col):
        pl.semaphore_signal(
            barrier, inc=1, device_id=(row, lax.rem(col + k, n_col)), device_id_type=MESH
        )
    for k in range(1, n_row):
        pl.semaphore_signal(
            barrier, inc=1, device_id=(lax.rem(row + k, n_row), col), device_id_type=MESH
        )

    zero_tile = jnp.zeros((c_lat, LANES), jnp.float32)
    for r in range(rp):
        tiles = [
            lat_ref[:, r * breadth + t * LANES : r * breadth + (t + 1) * LANES].astype(jnp.float32)
            for t in range(breadth // LANES)
        ]
        for c in range(n_col):
            start = c * TILE_W - 2
            t0 = start // LANES
            off = start - t0 * LANES
            lo = tiles[t0] if t0 >= 0 else zero_tile
            hi = tiles[t0 + 1] if t0 + 1 < len(tiles) else zero_tile
            both = pltpu.roll(jnp.concatenate([lo, hi], axis=1), 2 * LANES - off, 1)
            send[c, r * c_lat : (r + 1) * c_lat, :] = both[:, :LANES].astype(jnp.bfloat16)

    pl.semaphore_wait(barrier, n_col + n_row - 2)

    def rows(first, count):
        return pl.ds(pl.multiple_of(first * c_lat, c_lat), count * c_lat)

    mine = rows(2 + col * rp, rp)
    copies = []
    for k in range(1, n_col):
        target = lax.rem(col + k, n_col)
        copy = pltpu.make_async_remote_copy(
            src_ref=send.at[target],
            dst_ref=x_ref.at[mine],
            send_sem=send_sem.at[k],
            recv_sem=recv_sem.at[k],
            device_id=(row, target),
            device_id_type=MESH,
        )
        copy.start()
        copies.append(copy)
    x_ref[mine, :] = send[col]

    @pl.when(row == 0)
    def _():
        x_ref[rows(0, 2), :] = jnp.zeros((2 * c_lat, LANES), jnp.bfloat16)

    @pl.when(row == n_row - 1)
    def _():
        x_ref[rows(tile_h + 2, 2), :] = jnp.zeros((2 * c_lat, LANES), jnp.bfloat16)

    for copy in copies:
        copy.wait_recv()

    down = pltpu.make_async_remote_copy(
        src_ref=x_ref.at[rows(tile_h, 2)],
        dst_ref=x_ref.at[rows(0, 2)],
        send_sem=halo_send.at[0],
        recv_sem=halo_recv.at[0],
        device_id=(jnp.minimum(row + 1, n_row - 1), col),
        device_id_type=MESH,
    )
    up = pltpu.make_async_remote_copy(
        src_ref=x_ref.at[rows(2, 2)],
        dst_ref=x_ref.at[rows(tile_h + 2, 2)],
        send_sem=halo_send.at[1],
        recv_sem=halo_recv.at[1],
        device_id=(jnp.maximum(row - 1, 0), col),
        device_id_type=MESH,
    )

    @pl.when(row < n_row - 1)
    def _():
        down.start()

    @pl.when(row > 0)
    def _():
        up.start()

    def spread(i):
        src = x_ref[rows(i, 1), :].astype(jnp.float32)
        for b in range(3):
            moved = src if b == 0 else pltpu.roll(src, LANES - b, 1)
            xs_ref[rows(3 * i + b, 1), :] = moved.astype(jnp.bfloat16)

    def spread_loop(i, carry):
        for u in range(4):
            spread(2 + i * 4 + u)
        return carry

    lax.fori_loop(0, tile_h // 4, spread_loop, 0)

    cell = lax.broadcasted_iota(jnp.int32, (COLS_PAD, 1), 0)
    inside = jnp.logical_and(cell >= 1, cell <= TILE_W)
    weight = w_ref[...]
    bias = bias_ref[...]
    channels = weight.shape[1]

    def conv_row(i):
        patch = xs_ref[rows(3 * i, 9), :]
        out = lax.dot_general(
            patch, weight, (((0,), (0,)), ((), ())), preferred_element_type=jnp.float32
        )[:COLS_PAD]
        out = (out + bias).astype(jnp.bfloat16)
        fo_ref[i] = out
        return out

    def stats_row(i, carry):
        total, squares = carry
        out = jnp.where(inside, conv_row(i).astype(jnp.float32), 0.0)
        grouped = out.reshape(COLS_PAD // 8, 8, channels)
        return total + jnp.sum(grouped, axis=0), squares + jnp.sum(grouped * grouped, axis=0)

    def stats_pair(i, carry):
        return stats_row(3 + 2 * i, stats_row(2 + 2 * i, carry))

    zero = jnp.zeros((8, channels), jnp.float32)
    carry = lax.fori_loop(0, (tile_h - 2) // 2, stats_pair, (zero, zero))

    @pl.when(row < n_row - 1)
    def _():
        up.wait_recv()

    @pl.when(row > 0)
    def _():
        down.wait_recv()

    for i in (0, 1, tile_h + 2, tile_h + 3):
        spread(i)
    carry = stats_row(tile_h, stats_row(1, carry))
    part[0:1, :] = jnp.sum(carry[0], axis=0, keepdims=True)
    part[1:2, :] = jnp.sum(carry[1], axis=0, keepdims=True)

    firsts = []
    for k in range(1, n_col):
        copy = pltpu.make_async_remote_copy(
            src_ref=part, dst_ref=slot_col.at[k], send_sem=s1_send.at[k],
            recv_sem=s1_recv.at[k],
            device_id=(row, lax.rem(col + k, n_col)), device_id_type=MESH,
        )
        copy.start()
        firsts.append(copy)
    conv_row(0)
    conv_row(tile_h + 1)
    acc = part[...]
    for k, copy in enumerate(firsts):
        copy.wait_recv()
        acc = acc + slot_col[k + 1]
    part_row[...] = acc
    seconds = []
    for k in range(1, n_row):
        copy = pltpu.make_async_remote_copy(
            src_ref=part_row, dst_ref=slot_row.at[k], send_sem=s2_send.at[k],
            recv_sem=s2_recv.at[k],
            device_id=(lax.rem(row + k, n_row), col), device_id_type=MESH,
        )
        copy.start()
        seconds.append(copy)
    for k, copy in enumerate(seconds):
        copy.wait_recv()
        acc = acc + slot_row[k + 1]

    width = channels // GROUPS
    left = lax.broadcasted_iota(jnp.int32, (channels, channels), 0) // width
    right = lax.broadcasted_iota(jnp.int32, (channels, channels), 1) // width
    same = (left == right).astype(jnp.float32)
    padded = jnp.concatenate([acc, jnp.zeros((6, channels), jnp.float32)], axis=0)
    summed = jnp.dot(
        padded, same, precision=lax.Precision.HIGHEST, preferred_element_type=jnp.float32
    )
    cells = float(tile_h * TILE_W * n_row * n_col * width)
    mean = summed[0:1] / cells
    var = summed[1:2] / cells - mean * mean
    scale = lax.rsqrt(var + EPSILON) * gain_ref[...]
    ss_ref[0:1, :] = scale
    ss_ref[1:2, :] = shift_ref[...] - mean * scale

    for copy in copies + firsts + seconds:
        copy.wait_send()

    @pl.when(row < n_row - 1)
    def _():
        down.wait_send()

    @pl.when(row > 0)
    def _():
        up.wait_send()


def mid_kernel(n_row, n_col, tile_h, fo_ref, ss_ref, w_ref, bias_ref, out_ref, act_ref):
    row, col = lax.axis_index("row"), lax.axis_index("col")
    step = pl.program_id(0)
    channels = fo_ref.shape[2]
    scale = ss_ref[0:1, :] * 0.5
    shift = ss_ref[1:2, :] * 0.5
    cell = lax.broadcasted_iota(jnp.int32, (COLS_PAD, 1), 0)
    lowest = jnp.where(col == 0, 1, 0)
    highest = jnp.where(col == n_col - 1, TILE_W, TILE_W + 1)
    inside = jnp.logical_and(cell >= lowest, cell <= highest)

    def activate(i):
        half = fo_ref[i].astype(jnp.float32) * scale + shift
        value = half + half * jnp.tanh(half)
        beyond = jnp.logical_or(
            jnp.logical_and(row == 0, i == 0),
            jnp.logical_and(row == n_row - 1, i == tile_h + 1),
        )
        value = jnp.where(jnp.logical_and(inside, jnp.logical_not(beyond)), value, 0.0)
        first = pl.multiple_of(i * TILE_W, TILE_W)
        for b in range(3):
            moved = value if b == 0 else pltpu.roll(value, COLS_PAD - b, 0)
            act_ref[pl.ds(first, TILE_W), b * channels : (b + 1) * channels] = moved[
                :TILE_W
            ].astype(jnp.bfloat16)

    @pl.when(step == 0)
    def _():
        activate(0)
        activate(1)

    for u in range(ROWS_STEP):
        activate(step * ROWS_STEP + 2 + u)

    rows_m = ROWS_STEP * TILE_W
    acc = None
    for a in range(3):
        lhs = act_ref[pl.ds(pl.multiple_of((step * ROWS_STEP + a) * TILE_W, TILE_W), rows_m), :]
        rhs = jnp.concatenate([w_ref[3 * a + b] for b in range(3)], axis=1)
        prod = lax.dot_general(
            lhs, rhs, (((1,), (1,)), ((), ())), preferred_element_type=jnp.float32
        )
        acc = prod if acc is None else acc + prod
    out_ref[...] = (acc + bias_ref[...]).astype(jnp.bfloat16).reshape(out_ref.shape)


def body(n_row, n_col, latent, in_weight, in_bias, norm_gain, norm_shift, mid_weight, mid_bias):
    c_lat = latent.shape[0]
    channels = in_bias.shape[0]
    rp = latent.shape[1] // (TILE_W * n_col)
    tile_h = rp * n_col
    vmem = pl.BlockSpec(memory_space=pltpu.VMEM)
    dma = pltpu.SemaphoreType.DMA
    fo, ss = pl.pallas_call(
        functools.partial(front_kernel, n_row, n_col),
        out_shape=(
            jax.ShapeDtypeStruct((tile_h + 2, COLS_PAD, channels), jnp.bfloat16),
            jax.ShapeDtypeStruct((2, channels), jnp.float32),
        ),
        in_specs=[vmem] * 5,
        out_specs=(vmem, vmem),
        scratch_shapes=[
            pltpu.VMEM((n_col, rp * c_lat, LANES), jnp.bfloat16),
            pltpu.VMEM(((tile_h + 4) * c_lat, LANES), jnp.bfloat16),
            pltpu.VMEM(((tile_h + 4) * 3 * c_lat, LANES), jnp.bfloat16),
            pltpu.VMEM((2, channels), jnp.float32),
            pltpu.VMEM((n_col, 2, channels), jnp.float32),
            pltpu.VMEM((2, channels), jnp.float32),
            pltpu.VMEM((n_row, 2, channels), jnp.float32),
            dma((n_col,)), dma((n_col,)), dma((2,)), dma((2,)),
            dma((n_col,)), dma((n_col,)), dma((n_row,)), dma((n_row,)),
        ],
        compiler_params=pltpu.CompilerParams(
            collective_id=0, has_side_effects=True, vmem_limit_bytes=32 * 2**20
        ),
    )(
        latent,
        in_weight.reshape(9 * c_lat, channels),
        in_bias.reshape(1, channels),
        norm_gain.reshape(1, channels),
        norm_shift.reshape(1, channels),
    )
    weight = jnp.transpose(mid_weight, (1, 2, 0, 3)).reshape(9, channels, channels)
    whole = lambda *shape: pl.BlockSpec(shape, lambda s: (0,) * len(shape))
    return pl.pallas_call(
        functools.partial(mid_kernel, n_row, n_col, tile_h),
        grid=(tile_h // ROWS_STEP,),
        out_shape=jax.ShapeDtypeStruct((tile_h, TILE_W, channels), jnp.bfloat16),
        in_specs=[
            whole(tile_h + 2, COLS_PAD, channels),
            whole(2, channels),
            whole(9, channels, channels),
            whole(1, channels),
        ],
        out_specs=pl.BlockSpec((ROWS_STEP, TILE_W, channels), lambda s: (s, 0, 0)),
        scratch_shapes=[pltpu.VMEM(((tile_h + 2) * TILE_W, 3 * channels), jnp.bfloat16)],
        compiler_params=pltpu.CompilerParams(vmem_limit_bytes=56 * 2**20),
        cost_estimate=pl.CostEstimate(
            flops=2 * tile_h * TILE_W * 9 * channels * channels,
            bytes_accessed=14 * 2**20, transcendentals=0,
        ),
    )(fo, ss, weight, mid_bias.reshape(1, channels))


def solution(mesh):
    placed = (P(None, ("row", "col")), P(), P(), P(), P(), P(), P())
    return jax.shard_map(
        functools.partial(body, mesh.shape["row"], mesh.shape["col"]),
        mesh=mesh, in_specs=placed, out_specs=P("row", "col", None), check_vma=False,
    )
```

profile of v0, /device:TPU:0, one launch (start us, length us, event | category | flops | bytes accessed | tf_op | source)
XLA Modules:
  0.0 69.1 jit_solution(4616726618890479700)
XLA Ops:
  0.0 0.0 copy-start
  0.0 0.9 %copy-done = bf16[3,3,16,512]{3,2,1,0:T(8,128)(2,1)S(1)} copy-done((bf16[3,3,16,512]{3,2,1,0:T(8,128)(2,1)S(1)}, bf16[3,3,16,512]{3,2,1,0:T(8,128)(2,1)}, u32[]{:S(2)}) %copy-start) | copy-done | bytes 147480
  0.9 0.0 copy-start.1
  0.9 0.9 %copy-done.1 = bf16[16,4096]{1,0:T(8,128)(2,1)S(1)} copy-done((bf16[16,4096]{1,0:T(8,128)(2,1)S(1)}, bf16[16,4096]{1,0:T(8,128)(2,1)}, u32[]{:S(2)}) %copy-start.1) | copy-done | bytes 131096
  1.8 0.0 copy-start.2
  1.8 0.7 copy-done.2
  2.5 0.0 copy-start.3
  2.5 0.7 copy-done.3
  3.2 0.0 copy-start.4
  3.2 0.7 copy-done.4
  3.9 31.1 %shard_map.73 = (bf16[66,80,512]{2,1,0:T(8,128)(2,1)S(1)}, f32[2,512]{1,0:T(2,128)S(1)}) custom-call(bf16[16,4096]{1,0:T(8,128)(2,1)S(1)} %copy-done.1, bf16[144,512]{1,0:T(8,128)(2,1)S(1)} %bitcast.8, f32[1,512]{1,0:T(1,128)S(1)} %bitcast.9, f32[1,512]{1,0:T(1,128)S(1)} %bitcast.10, f32[1,512]{1,0:T(1,128)S(1)} %bitcast.11), custom_call_target="tpu_custom_call" | custom-call | tf_op jit(solution)/shard_map/pallas_call | solution.py:276
  35.0 0.0 copy-start.5
  35.0 2.3 %copy-done.5 = bf16[66,80,512]{2,1,0:T(8,128)(2,1)} copy-done((bf16[66,80,512]{2,1,0:T(8,128)(2,1)}, bf16[66,80,512]{2,1,0:T(8,128)(2,1)S(1)}, u32[]{:S(2)}) %copy-start.5) | copy-done | bytes 5406744
  37.3 0.0 copy-start.6
  37.3 0.6 copy-done.6
  37.9 31.2 %shard_map.74 = bf16[64,64,512]{2,1,0:T(8,128)(2,1)} custom-call(bf16[66,80,512]{2,1,0:T(8,128)(2,1)} %copy-done.5, f32[2,512]{1,0:T(2,128)} %copy-done.6, bf16[9,512,512]{2,1,0:T(8,128)(2,1)} %bitcast.12, f32[1,512]{1,0:T(1,128)} %bitcast.13), custom_call_target="tpu_custom_call" | custom-call | flops 19327352832 | bytes 14680064 | tf_op jit(solution)/shard_map/pallas_call | solution.py:307
Async XLA Ops:
  0.0 0.9 %copy-start = (bf16[3,3,16,512]{3,2,1,0:T(8,128)(2,1)S(1)}, bf16[3,3,16,512]{3,2,1,0:T(8,128)(2,1)}, u32[]{:S(2)}) copy-start(bf16[3,3,16,512]{3,2,1,0:T(8,128)(2,1)} %param.8) | copy-start | bytes 442372
  0.9 0.9 %copy-start.1 = (bf16[16,4096]{1,0:T(8,128)(2,1)S(1)}, bf16[16,4096]{1,0:T(8,128)(2,1)}, u32[]{:S(2)}) copy-start(bf16[16,4096]{1,0:T(8,128)(2,1)} %lat_ref.1) | copy-start | bytes 393220
  1.8 0.7 copy-start.2
  2.5 0.7 copy-start.3
  3.2 0.7 copy-start.4
  35.0 2.3 %copy-start.5 = (bf16[66,80,512]{2,1,0:T(8,128)(2,1)}, bf16[66,80,512]{2,1,0:T(8,128)(2,1)S(1)}, u32[]{:S(2)}) copy-start(bf16[66,80,512]{2,1,0:T(8,128)(2,1)S(1)} %get-tuple-element.7.fo_ref) | copy-start | bytes 16220164
  37.3 0.6 copy-start.6
where the time goes:
time: 69.3 us; the launch traced here: 69.1 us
  Pallas kernels  62.3 us (90%)
  local copies, waits for them, and re-layouts  6.78 us (10%)
    pallas_call x1, Pallas kernels, body(): pl.pallas_call(functools.partial(mid_kernel, n_row, n_col, tile_h), grid=...  31.2 us
    pallas_call x1, Pallas kernels, body(): pl.pallas_call(functools.partial(front_kernel, n_row, n_col), out_shape=(...  31.1 us
    unnamed x14, local copies, waits for them, and re-layouts  6.78 us

commit v1 on v0

--- a/solution.py
+++ b/solution.py
@@ -13,16 +13,28 @@
 LANES = 128
 MESH = pl.DeviceIdType.MESH
 COLS_PAD = 80
-ROWS_STEP = 4
-
-
-def front_kernel(
-    n_row, n_col, lat_ref, w_ref, bias_ref, gain_ref, shift_ref,
-    fo_ref, ss_ref,
+COLS_USED = 72
+ROWS_STEP = 8
+
+
+def kernel(
+    n_row, n_col, lat_hbm, w_hbm, bias_hbm, gain_hbm, shift_hbm, mid_hbm, mid_bias_hbm,
+    out_hbm,
+    fo_ref, ss_ref, mid_ref, out_ref, even_ref, odd_ref, out_sem,
+    lat_ref, w_ref, bias_ref, gain_ref, shift_ref, mid_bias_ref, fetch_sem,
     send, x_ref, xs_ref, part, slot_col, part_row, slot_row,
     send_sem, recv_sem, halo_send, halo_recv, s1_send, s1_recv, s2_send, s2_recv,
 ):
     row, col = lax.axis_index("row"), lax.axis_index("col")
+    fetches = [
+        pltpu.make_async_copy(src, dst, fetch_sem.at[i])
+        for i, (src, dst) in enumerate([
+            (lat_hbm, lat_ref), (w_hbm, w_ref), (bias_hbm, bias_ref), (gain_hbm, gain_ref),
+            (shift_hbm, shift_ref), (mid_bias_hbm, mid_bias_ref), (mid_hbm, mid_ref),
+        ])
+    ]
+    for fetch in fetches:
+        fetch.start()
     c_lat = lat_ref.shape[0]
     breadth = TILE_W * n_col
     rp = lat_ref.shape[1] // breadth
@@ -38,6 +50,7 @@
             barrier, inc=1, device_id=(lax.rem(row + k, n_row), col), device_id_type=MESH
         )
 
+    fetches[0].wait()
     zero_tile = jnp.zeros((c_lat, LANES), jnp.float32)
     for r in range(rp):
         tiles = [
@@ -123,6 +136,8 @@
 
     lax.fori_loop(0, tile_h // 4, spread_loop, 0)
 
+    fetches[1].wait()
+    fetches[2].wait()
     cell = lax.broadcasted_iota(jnp.int32, (COLS_PAD, 1), 0)
     inside = jnp.logical_and(cell >= 1, cell <= TILE_W)
     weight = w_ref[...]
@@ -164,6 +179,8 @@
     part[0:1, :] = jnp.sum(carry[0], axis=0, keepdims=True)
     part[1:2, :] = jnp.sum(carry[1], axis=0, keepdims=True)
 
+    for fetch in fetches[3:]:
+        fetch.wait()
     firsts = []
     for k in range(1, n_col):
         copy = pltpu.make_async_remote_copy(
@@ -207,6 +224,10 @@
     scale = lax.rsqrt(var + EPSILON) * gain_ref[...]
     ss_ref[0:1, :] = scale
     ss_ref[1:2, :] = shift_ref[...] - mean * scale
+    mid_conv(
+        n_row, n_col, tile_h, fo_ref, ss_ref, mid_ref, mid_bias_ref, out_ref, out_hbm,
+        even_ref, odd_ref, out_sem,
+    )
 
     for copy in copies + firsts + seconds:
         copy.wait_send()
@@ -220,50 +241,70 @@
         up.wait_send()
 
 
-def mid_kernel(n_row, n_col, tile_h, fo_ref, ss_ref, w_ref, bias_ref, out_ref, act_ref):
+def mid_conv(
+    n_row, n_col, tile_h, fo_ref, ss_ref, w_ref, bias_ref, out_ref, out_hbm,
+    even_ref, odd_ref, out_sem,
+):
     row, col = lax.axis_index("row"), lax.axis_index("col")
-    step = pl.program_id(0)
     channels = fo_ref.shape[2]
     scale = ss_ref[0:1, :] * 0.5
     shift = ss_ref[1:2, :] * 0.5
-    cell = lax.broadcasted_iota(jnp.int32, (COLS_PAD, 1), 0)
+    bias = bias_ref[...]
+    cell = lax.broadcasted_iota(jnp.int32, (COLS_USED, 1), 0)
     lowest = jnp.where(col == 0, 1, 0)
     highest = jnp.where(col == n_col - 1, TILE_W, TILE_W + 1)
-    inside = jnp.logical_and(cell >= lowest, cell <= highest)
-
-    def activate(i):
-        half = fo_ref[i].astype(jnp.float32) * scale + shift
+
+    def activate(i, act_ref, slot):
+        half = fo_ref[i, :COLS_USED].astype(jnp.float32) * scale + shift
         value = half + half * jnp.tanh(half)
         beyond = jnp.logical_or(
             jnp.logical_and(row == 0, i == 0),
             jnp.logical_and(row == n_row - 1, i == tile_h + 1),
         )
-        value = jnp.where(jnp.logical_and(inside, jnp.logical_not(beyond)), value, 0.0)
-        first = pl.multiple_of(i * TILE_W, TILE_W)
+        last = jnp.where(beyond, -1, highest)
+        value = jnp.where(jnp.logical_and(cell >= lowest, cell <= last), value, 0.0)
         for b in range(3):
-            moved = value if b == 0 else pltpu.roll(value, COLS_PAD - b, 0)
-            act_ref[pl.ds(first, TILE_W), b * channels : (b + 1) * channels] = moved[
-                :TILE_W
-            ].astype(jnp.bfloat16)
-
-    @pl.when(step == 0)
-    def _():
-        activate(0)
-        activate(1)
-
-    for u in range(ROWS_STEP):
-        activate(step * ROWS_STEP + 2 + u)
+            moved = value if b == 0 else pltpu.roll(value, COLS_USED - b, 0)
+            act_ref[slot * TILE_W : (slot + 1) * TILE_W, b * channels : (b + 1) * channels] = (
+                moved[:TILE_W].astype(jnp.bfloat16)
+            )
+
+    for i in range(ROWS_STEP + 2):
+        activate(i, even_ref, i)
 
     rows_m = ROWS_STEP * TILE_W
-    acc = None
-    for a in range(3):
-        lhs = act_ref[pl.ds(pl.multiple_of((step * ROWS_STEP + a) * TILE_W, TILE_W), rows_m), :]
-        rhs = jnp.concatenate([w_ref[3 * a + b] for b in range(3)], axis=1)
-        prod = lax.dot_general(
-            lhs, rhs, (((1,), (1,)), ((), ())), preferred_element_type=jnp.float32
-        )
-        acc = prod if acc is None else acc + prod
-    out_ref[...] = (acc + bias_ref[...]).astype(jnp.bfloat16).reshape(out_ref.shape)
+    blocks = tile_h // ROWS_STEP
+
+    def leave(block):
+        part = pl.ds(block * ROWS_STEP, ROWS_STEP)
+        return pltpu.make_async_copy(out_ref.at[part], out_hbm.at[part], out_sem.at[block])
+
+    def two_blocks(step, carry):
+        for half_step, (now, later) in enumerate(((even_ref, odd_ref), (odd_ref, even_ref))):
+            first = (2 * step + half_step + 1) * ROWS_STEP
+            later[: 2 * TILE_W, :] = now[rows_m:, :]
+            acc = None
+            done = 0
+            for a in range(3):
+                rhs = jnp.concatenate([w_ref[3 * a + b] for b in range(3)], axis=1)
+                prod = lax.dot_general(
+                    now[a * TILE_W : a * TILE_W + rows_m, :], rhs, (((1,), (1,)), ((), ())),
+                    preferred_element_type=jnp.float32,
+                )
+                upto = ((a + 1) * ROWS_STEP) // 3
+                for u in range(done, upto):
+                    activate(jnp.minimum(first + 2 + u, tile_h + 1), later, 2 + u)
+                done = upto
+                acc = prod if acc is None else acc + prod
+            out_ref[pl.ds(first - ROWS_STEP, ROWS_STEP)] = (
+                (acc + bias).astype(jnp.bfloat16).reshape(ROWS_STEP, TILE_W, channels)
+            )
+            leave(2 * step + half_step).start()
+        return carry
+
+    lax.fori_loop(0, blocks // 2, two_blocks, 0)
+    for block in range(blocks):
+        leave(block).wait()
 
 
 def body(n_row, n_col, latent, in_weight, in_bias, norm_gain, norm_shift, mid_weight, mid_bias):
@@ -271,17 +312,26 @@
     channels = in_bias.shape[0]
     rp = latent.shape[1] // (TILE_W * n_col)
     tile_h = rp * n_col
-    vmem = pl.BlockSpec(memory_space=pltpu.VMEM)
     dma = pltpu.SemaphoreType.DMA
-    fo, ss = pl.pallas_call(
-        functools.partial(front_kernel, n_row, n_col),
-        out_shape=(
-            jax.ShapeDtypeStruct((tile_h + 2, COLS_PAD, channels), jnp.bfloat16),
-            jax.ShapeDtypeStruct((2, channels), jnp.float32),
-        ),
-        in_specs=[vmem] * 5,
-        out_specs=(vmem, vmem),
+    vector = pltpu.VMEM((1, channels), jnp.float32)
+    weight = jnp.transpose(mid_weight, (1, 2, 0, 3)).reshape(9, channels, channels)
+    act = pltpu.VMEM(((ROWS_STEP + 2) * TILE_W, 3 * channels), jnp.bfloat16)
+    out_shape = (tile_h, TILE_W, channels)
+    hbm = pl.BlockSpec(memory_space=pltpu.HBM)
+    return pl.pallas_call(
+        functools.partial(kernel, n_row, n_col),
+        out_shape=jax.ShapeDtypeStruct(out_shape, jnp.bfloat16),
+        in_specs=[hbm] * 7,
+        out_specs=hbm,
         scratch_shapes=[
+            pltpu.VMEM((tile_h + 2, COLS_PAD, channels), jnp.bfloat16),
+            pltpu.VMEM((8, channels), jnp.float32),
+            pltpu.VMEM(weight.shape, jnp.bfloat16),
+            pltpu.VMEM(out_shape, jnp.bfloat16),
+            act, act, dma((tile_h // ROWS_STEP,)),
+            pltpu.VMEM(latent.shape, jnp.bfloat16),
+            pltpu.VMEM((9 * c_lat, channels), jnp.bfloat16),
+            vector, vector, vector, vector, dma((7,)),
             pltpu.VMEM((n_col, rp * c_lat, LANES), jnp.bfloat16),
             pltpu.VMEM(((tile_h + 4) * c_lat, LANES), jnp.bfloat16),
             pltpu.VMEM(((tile_h + 4) * 3 * c_lat, LANES), jnp.bfloat16),
@@ -293,7 +343,11 @@
             dma((n_col,)), dma((n_col,)), dma((n_row,)), dma((n_row,)),
         ],
         compiler_params=pltpu.CompilerParams(
-            collective_id=0, has_side_effects=True, vmem_limit_bytes=32 * 2**20
+            collective_id=0, has_side_effects=True, vmem_limit_bytes=63 * 2**20
+        ),
+        cost_estimate=pl.CostEstimate(
+            flops=2 * tile_h * TILE_W * 9 * channels * channels,
+            bytes_accessed=10 * 2**20, transcendentals=0,
         ),
     )(
         latent,
@@ -301,27 +355,9 @@
         in_bias.reshape(1, channels),
         norm_gain.reshape(1, channels),
         norm_shift.reshape(1, channels),
-    )
-    weight = jnp.transpose(mid_weight, (1, 2, 0, 3)).reshape(9, channels, channels)
-    whole = lambda *shape: pl.BlockSpec(shape, lambda s: (0,) * len(shape))
-    return pl.pallas_call(
-        functools.partial(mid_kernel, n_row, n_col, tile_h),
-        grid=(tile_h // ROWS_STEP,),
-        out_shape=jax.ShapeDtypeStruct((tile_h, TILE_W, channels), jnp.bfloat16),
-        in_specs=[
-            whole(tile_h + 2, COLS_PAD, channels),
-            whole(2, channels),
-            whole(9, channels, channels),
-            whole(1, channels),
-        ],
-        out_specs=pl.BlockSpec((ROWS_STEP, TILE_W, channels), lambda s: (s, 0, 0)),
-        scratch_shapes=[pltpu.VMEM(((tile_h + 2) * TILE_W, 3 * channels), jnp.bfloat16)],
-        compiler_params=pltpu.CompilerParams(vmem_limit_bytes=56 * 2**20),
-        cost_estimate=pl.CostEstimate(
-            flops=2 * tile_h * TILE_W * 9 * channels * channels,
-            bytes_accessed=14 * 2**20, transcendentals=0,
-        ),
-    )(fo, ss, weight, mid_bias.reshape(1, channels))
+        weight,
+        mid_bias.reshape(1, channels),
+    )
 
 
 def solution(mesh):

time: 69.3 us -> 58.1 us (0.84)
  Pallas kernels: 62.3 us -> 53.2 us
  local copies, waits for them, and re-layouts: 6.78 us -> 4.7 us
    pallas_call x2 -> x1, Pallas kernels: 62.3 us -> 53.2 us  [body(): pl.pallas_call(functools.partial(kernel, n_row, n_col), out_shape=jax.Sha...]
    unnamed x14 -> x1, local copies, waits for them, and re-layouts: 6.78 us -> 4.7 us
where the time goes in v1:
time: 58.1 us; the launch traced here: 58 us
  Pallas kernels  53.2 us (92%)
  local copies, waits for them, and re-layouts  4.7 us (8%)
    pallas_call x1, Pallas kernels, body(): pl.pallas_call(functools.partial(kernel, n_row, n_col), out_shape=jax.Sha...  53.2 us
    unnamed x1, local copies, waits for them, and re-layouts  4.7 us

profile of v1, /device:TPU:0, one launch (start us, length us, event | category | flops | bytes accessed | tf_op | source)
XLA Modules:
  0.0 58.0 jit_solution(2078165056762586001)
XLA Ops:
  0.0 53.2 %shard_map.73 = bf16[64,64,512]{2,1,0:T(8,128)(2,1)} custom-call(bf16[16,4096]{1,0:T(8,128)(2,1)} %lat_hbm.1, bf16[144,512]{1,0:T(8,128)(2,1)} %bitcast.9, f32[1,512]{1,0:T(1,128)} %bitcast.10, f32[1,512]{1,0:T(1,128)} %bitcast.11, f32[1,512]{1,0:T(1,128)} %bitcast.12, bf16[9,512,512]{2,1,0:T(8,128)(2,1)} %bitcast.8, f32[1,512]{1,0:T(1,128)} %bitcast.13), custom_call_target="tpu_custom_call" | custom-call | flops 19327352832 | bytes 10485760 | tf_op jit(solution)/shard_map/pallas_call | solution.py:321
  53.3 4.7 %copy.9 = bf16[64,64,512]{2,1,0:T(8,128)(2,1)} copy(bf16[64,64,512]{2,1,0:T(8,128)(2,1)} %shard_map.73) | data formatting | bytes 8388608

commit v2 on v1

--- a/solution.py
+++ b/solution.py
@@ -17,11 +17,11 @@
 ROWS_STEP = 8
 
 
-def kernel(
-    n_row, n_col, lat_hbm, w_hbm, bias_hbm, gain_hbm, shift_hbm, mid_hbm, mid_bias_hbm,
-    out_hbm,
-    fo_ref, ss_ref, mid_ref, out_ref, even_ref, odd_ref, out_sem,
-    lat_ref, w_ref, bias_ref, gain_ref, shift_ref, mid_bias_ref, fetch_sem,
+def front_kernel(
+    n_row, n_col, lat_hbm, w_hbm, bias_hbm, gain_hbm, shift_hbm,
+    fo_hbm, ss_hbm,
+    fo_ref, ss_ref, same_ref, leave_sem,
+    lat_ref, w_ref, bias_ref, gain_ref, shift_ref, fetch_sem,
     send, x_ref, xs_ref, part, slot_col, part_row, slot_row,
     send_sem, recv_sem, halo_send, halo_recv, s1_send, s1_recv, s2_send, s2_recv,
 ):
@@ -30,7 +30,7 @@
         pltpu.make_async_copy(src, dst, fetch_sem.at[i])
         for i, (src, dst) in enumerate([
             (lat_hbm, lat_ref), (w_hbm, w_ref), (bias_hbm, bias_ref), (gain_hbm, gain_ref),
-            (shift_hbm, shift_ref), (mid_bias_hbm, mid_bias_ref), (mid_hbm, mid_ref),
+            (shift_hbm, shift_ref),
         ])
     ]
     for fetch in fetches:
@@ -95,8 +95,20 @@
     def _():
         x_ref[rows(tile_h + 2, 2), :] = jnp.zeros((2 * c_lat, LANES), jnp.bfloat16)
 
-    for copy in copies:
+    def spread(i):
+        src = x_ref[rows(i, 1), :].astype(jnp.float32)
+        for b in range(3):
+            moved = src if b == 0 else pltpu.roll(src, LANES - b, 1)
+            xs_ref[rows(3 * i + b, 1), :] = moved.astype(jnp.bfloat16)
+
+    def spread_block(source):
+        for u in range(rp):
+            spread(2 + source * rp + u)
+
+    spread_block(col)
+    for k, copy in enumerate(copies):
         copy.wait_recv()
+        spread_block(lax.rem(col + n_col - k - 1, n_col))
 
     down = pltpu.make_async_remote_copy(
         src_ref=x_ref.at[rows(tile_h, 2)],
@@ -123,19 +135,6 @@
     def _():
         up.start()
 
-    def spread(i):
-        src = x_ref[rows(i, 1), :].astype(jnp.float32)
-        for b in range(3):
-            moved = src if b == 0 else pltpu.roll(src, LANES - b, 1)
-            xs_ref[rows(3 * i + b, 1), :] = moved.astype(jnp.bfloat16)
-
-    def spread_loop(i, carry):
-        for u in range(4):
-            spread(2 + i * 4 + u)
-        return carry
-
-    lax.fori_loop(0, tile_h // 4, spread_loop, 0)
-
     fetches[1].wait()
     fetches[2].wait()
     cell = lax.broadcasted_iota(jnp.int32, (COLS_PAD, 1), 0)
@@ -144,23 +143,29 @@
     bias = bias_ref[...]
     channels = weight.shape[1]
 
-    def conv_row(i):
-        patch = xs_ref[rows(3 * i, 9), :]
-        out = lax.dot_general(
-            patch, weight, (((0,), (0,)), ((), ())), preferred_element_type=jnp.float32
-        )[:COLS_PAD]
-        out = (out + bias).astype(jnp.bfloat16)
-        fo_ref[i] = out
-        return out
-
-    def stats_row(i, carry):
+    def conv_rows(indices):
+        patches = jnp.concatenate([xs_ref[rows(3 * i, 9), :] for i in indices], axis=1)
+        prod = lax.dot_general(
+            patches, weight, (((0,), (0,)), ((), ())), preferred_element_type=jnp.float32
+        )
+        outs = []
+        for u, i in enumerate(indices):
+            out = (prod[u * LANES : u * LANES + COLS_PAD] + bias).astype(jnp.bfloat16)
+            fo_ref[i] = out
+            outs.append(out)
+        return outs
+
+    def stats_rows(indices, carry):
         total, squares = carry
-        out = jnp.where(inside, conv_row(i).astype(jnp.float32), 0.0)
-        grouped = out.reshape(COLS_PAD // 8, 8, channels)
-        return total + jnp.sum(grouped, axis=0), squares + jnp.sum(grouped * grouped, axis=0)
+        for out in conv_rows(indices):
+            out = jnp.where(inside, out.astype(jnp.float32), 0.0)
+            grouped = out.reshape(COLS_PAD // 8, 8, channels)
+            total = total + jnp.sum(grouped, axis=0)
+            squares = squares + jnp.sum(grouped * grouped, axis=0)
+        return total, squares
 
     def stats_pair(i, carry):
-        return stats_row(3 + 2 * i, stats_row(2 + 2 * i, carry))
+        return stats_rows([2 + 2 * i, 3 + 2 * i], carry)
 
     zero = jnp.zeros((8, channels), jnp.float32)
     carry = lax.fori_loop(0, (tile_h - 2) // 2, stats_pair, (zero, zero))
@@ -175,7 +180,7 @@
 
     for i in (0, 1, tile_h + 2, tile_h + 3):
         spread(i)
-    carry = stats_row(tile_h, stats_row(1, carry))
+    carry = stats_rows([1, tile_h], carry)
     part[0:1, :] = jnp.sum(carry[0], axis=0, keepdims=True)
     part[1:2, :] = jnp.sum(carry[1], axis=0, keepdims=True)
 
@@ -190,8 +195,13 @@
         )
         copy.start()
         firsts.append(copy)
-    conv_row(0)
-    conv_row(tile_h + 1)
+    conv_rows([0, tile_h + 1])
+    leave_fo = pltpu.make_async_copy(fo_ref, fo_hbm, leave_sem.at[0])
+    leave_fo.start()
+    width = channels // GROUPS
+    left = lax.broadcasted_iota(jnp.int32, (channels, channels), 0) // width
+    right = lax.broadcasted_iota(jnp.int32, (channels, channels), 1) // width
+    same_ref[...] = (left == right).astype(jnp.bfloat16)
     acc = part[...]
     for k, copy in enumerate(firsts):
         copy.wait_recv()
@@ -210,25 +220,28 @@
         copy.wait_recv()
         acc = acc + slot_row[k + 1]
 
-    width = channels // GROUPS
-    left = lax.broadcasted_iota(jnp.int32, (channels, channels), 0) // width
-    right = lax.broadcasted_iota(jnp.int32, (channels, channels), 1) // width
-    same = (left == right).astype(jnp.float32)
-    padded = jnp.concatenate([acc, jnp.zeros((6, channels), jnp.float32)], axis=0)
-    summed = jnp.dot(
-        padded, same, precision=lax.Precision.HIGHEST, preferred_element_type=jnp.float32
+    parts = []
+    rest = jnp.concatenate([acc, jnp.zeros((6, channels), jnp.float32)], axis=0)
+    for _ in range(3):
+        parts.append(rest.astype(jnp.bfloat16).astype(jnp.float32))
+        rest = rest - parts[-1]
+    parts.append(jnp.zeros_like(rest))
+    three = jnp.dot(
+        jnp.concatenate(parts, axis=0).astype(jnp.bfloat16), same_ref[...],
+        preferred_element_type=jnp.float32,
     )
+    summed = three[0:8] + three[8:16] + three[16:24]
     cells = float(tile_h * TILE_W * n_row * n_col * width)
     mean = summed[0:1] / cells
     var = summed[1:2] / cells - mean * mean
     scale = lax.rsqrt(var + EPSILON) * gain_ref[...]
+    ss_ref[...] = jnp.zeros_like(ss_ref)
     ss_ref[0:1, :] = scale
     ss_ref[1:2, :] = shift_ref[...] - mean * scale
-    mid_conv(
-        n_row, n_col, tile_h, fo_ref, ss_ref, mid_ref, mid_bias_ref, out_ref, out_hbm,
-        even_ref, odd_ref, out_sem,
-    )
-
+    leave_ss = pltpu.make_async_copy(ss_ref, ss_hbm, leave_sem.at[1])
+    leave_ss.start()
+    leave_fo.wait()
+    leave_ss.wait()
     for copy in copies + firsts + seconds:
         copy.wait_send()
 
@@ -241,10 +254,30 @@
         up.wait_send()
 
 
-def mid_conv(
-    n_row, n_col, tile_h, fo_ref, ss_ref, w_ref, bias_ref, out_ref, out_hbm,
-    even_ref, odd_ref, out_sem,
+def mid_kernel(
+    n_row, n_col, fo_hbm, ss_hbm, w_hbm, bias_hbm, out_hbm,
+    fo_ref, ss_ref, w_ref, bias_ref, out_ref, even_ref, odd_ref, in_sem, fo_sem, out_sem,
 ):
+    tile_h = out_ref.shape[0]
+    blocks = tile_h // ROWS_STEP
+
+    def bring(block):
+        part = pl.ds(block * ROWS_STEP + 2, ROWS_STEP)
+        return pltpu.make_async_copy(fo_hbm.at[part], fo_ref.at[part], fo_sem.at[block])
+
+    early = [
+        pltpu.make_async_copy(ss_hbm, ss_ref, in_sem.at[0]),
+        pltpu.make_async_copy(bias_hbm, bias_ref, in_sem.at[1]),
+        pltpu.make_async_copy(fo_hbm.at[pl.ds(0, 2)], fo_ref.at[pl.ds(0, 2)], in_sem.at[2]),
+        bring(0),
+    ]
+    fetch_w = pltpu.make_async_copy(w_hbm, w_ref, in_sem.at[3])
+    for copy in early + [fetch_w]:
+        copy.start()
+    for block in range(1, blocks):
+        bring(block).start()
+    for copy in early:
+        copy.wait()
     row, col = lax.axis_index("row"), lax.axis_index("col")
     channels = fo_ref.shape[2]
     scale = ss_ref[0:1, :] * 0.5
@@ -273,7 +306,7 @@
         activate(i, even_ref, i)
 
     rows_m = ROWS_STEP * TILE_W
-    blocks = tile_h // ROWS_STEP
+    fetch_w.wait()
 
     def leave(block):
         part = pl.ds(block * ROWS_STEP, ROWS_STEP)
@@ -282,6 +315,11 @@
     def two_blocks(step, carry):
         for half_step, (now, later) in enumerate(((even_ref, odd_ref), (odd_ref, even_ref))):
             first = (2 * step + half_step + 1) * ROWS_STEP
+
+            @pl.when(first < tile_h)
+            def _(block=2 * step + half_step + 1):
+                bring(block).wait()
+
             later[: 2 * TILE_W, :] = now[rows_m:, :]
             acc = None
             done = 0
@@ -318,20 +356,24 @@
     act = pltpu.VMEM(((ROWS_STEP + 2) * TILE_W, 3 * channels), jnp.bfloat16)
     out_shape = (tile_h, TILE_W, channels)
     hbm = pl.BlockSpec(memory_space=pltpu.HBM)
-    return pl.pallas_call(
-        functools.partial(kernel, n_row, n_col),
-        out_shape=jax.ShapeDtypeStruct(out_shape, jnp.bfloat16),
-        in_specs=[hbm] * 7,
-        out_specs=hbm,
+    fo_shape = (tile_h + 2, COLS_PAD, channels)
+    blocks = tile_h // ROWS_STEP
+    fo, ss = pl.pallas_call(
+        functools.partial(front_kernel, n_row, n_col),
+        out_shape=(
+            jax.ShapeDtypeStruct(fo_shape, jnp.bfloat16),
+            jax.ShapeDtypeStruct((8, channels), jnp.float32),
+        ),
+        in_specs=[hbm] * 5,
+        out_specs=(hbm, hbm),
         scratch_shapes=[
-            pltpu.VMEM((tile_h + 2, COLS_PAD, channels), jnp.bfloat16),
+            pltpu.VMEM(fo_shape, jnp.bfloat16),
             pltpu.VMEM((8, channels), jnp.float32),
-            pltpu.VMEM(weight.shape, jnp.bfloat16),
-            pltpu.VMEM(out_shape, jnp.bfloat16),
-            act, act, dma((tile_h // ROWS_STEP,)),
+            pltpu.VMEM((channels, channels), jnp.bfloat16),
+            dma((2,)),
             pltpu.VMEM(latent.shape, jnp.bfloat16),
             pltpu.VMEM((9 * c_lat, channels), jnp.bfloat16),
-            vector, vector, vector, vector, dma((7,)),
+            vector, vector, vector, dma((5,)),
             pltpu.VMEM((n_col, rp * c_lat, LANES), jnp.bfloat16),
             pltpu.VMEM(((tile_h + 4) * c_lat, LANES), jnp.bfloat16),
             pltpu.VMEM(((tile_h + 4) * 3 * c_lat, LANES), jnp.bfloat16),
@@ -345,19 +387,32 @@
         compiler_params=pltpu.CompilerParams(
             collective_id=0, has_side_effects=True, vmem_limit_bytes=63 * 2**20
         ),
-        cost_estimate=pl.CostEstimate(
-            flops=2 * tile_h * TILE_W * 9 * channels * channels,
-            bytes_accessed=10 * 2**20, transcendentals=0,
-        ),
     )(
         latent,
         in_weight.reshape(9 * c_lat, channels),
         in_bias.reshape(1, channels),
         norm_gain.reshape(1, channels),
         norm_shift.reshape(1, channels),
-        weight,
-        mid_bias.reshape(1, channels),
     )
+    return pl.pallas_call(
+        functools.partial(mid_kernel, n_row, n_col),
+        out_shape=jax.ShapeDtypeStruct(out_shape, jnp.bfloat16),
+        in_specs=[hbm] * 4,
+        out_specs=hbm,
+        scratch_shapes=[
+            pltpu.VMEM(fo_shape, jnp.bfloat16),
+            pltpu.VMEM((8, channels), jnp.float32),
+            pltpu.VMEM(weight.shape, jnp.bfloat16),
+            vector,
+            pltpu.VMEM(out_shape, jnp.bfloat16),
+            act, act, dma((4,)), dma((blocks,)), dma((blocks,)),
+        ],
+        compiler_params=pltpu.CompilerParams(vmem_limit_bytes=63 * 2**20),
+        cost_estimate=pl.CostEstimate(
+            flops=2 * tile_h * TILE_W * 9 * channels * channels,
+            bytes_accessed=14 * 2**20, transcendentals=0,
+        ),
+    )(fo, ss, weight, mid_bias.reshape(1, channels))
 
 
 def solution(mesh):

time: 58.1 us -> 58 us (level)
  local copies, waits for them, and re-layouts: 4.7 us -> 0 us
  Pallas kernels: 53.2 us -> 57.8 us
    unnamed x1 -> x0, local copies, waits for them, and re-layouts: 4.7 us -> none
    pallas_call x1 -> x2, Pallas kernels: 53.2 us -> 57.8 us  [the longest x1 30.5 us: body(): pl.pallas_call(functools.partial(front_kernel, n_row, n_col), out_shape=(...]
where the time goes in v2:
time: 58 us; the launch traced here: 57.8 us
  Pallas kernels  57.8 us (100%)
    pallas_call x1, Pallas kernels, body(): pl.pallas_call(functools.partial(front_kernel, n_row, n_col), out_shape=(...  30.5 us
    pallas_call x1, Pallas kernels, body(): pl.pallas_call(functools.partial(mid_kernel, n_row, n_col), out_shape=jax...  27.2 us

profile of v2, /device:TPU:0, one launch (start us, length us, event | category | flops | bytes accessed | tf_op | source)
XLA Modules:
  0.0 57.8 jit_solution(3040101528983649750)
XLA Ops:
  0.0 30.5 %shard_map.73 = (bf16[66,80,512]{2,1,0:T(8,128)(2,1)}, f32[8,512]{1,0:T(8,128)}) custom-call(bf16[16,4096]{1,0:T(8,128)(2,1)} %lat_hbm.1, bf16[144,512]{1,0:T(8,128)(2,1)} %bitcast.8, f32[1,512]{1,0:T(1,128)} %bitcast.9, f32[1,512]{1,0:T(1,128)} %bitcast.10, f32[1,512]{1,0:T(1,128)} %bitcast.11), custom_call_target="tpu_custom_call" | custom-call | tf_op jit(solution)/shard_map/pallas_call | solution.py:361
  30.6 27.2 %shard_map.74 = bf16[64,64,512]{2,1,0:T(8,128)(2,1)} custom-call(bf16[66,80,512]{2,1,0:T(8,128)(2,1)} %get-tuple-element.7.fo_hbm, f32[8,512]{1,0:T(8,128)} %get-tuple-element.8.ss_hbm, bf16[9,512,512]{2,1,0:T(8,128)(2,1)} %bitcast.12, f32[1,512]{1,0:T(1,128)} %bitcast.13), custom_call_target="tpu_custom_call" | custom-call | flops 19327352832 | bytes 14680064 | tf_op jit(solution)/shard_map/pallas_call | solution.py:397

commit v3 on v2

--- a/solution.py
+++ b/solution.py
@@ -164,11 +164,14 @@
             squares = squares + jnp.sum(grouped * grouped, axis=0)
         return total, squares
 
-    def stats_pair(i, carry):
-        return stats_rows([2 + 2 * i, 3 + 2 * i], carry)
+    def stats_four(i, carry):
+        return stats_rows([2 + 4 * i + u for u in range(4)], carry)
 
     zero = jnp.zeros((8, channels), jnp.float32)
-    carry = lax.fori_loop(0, (tile_h - 2) // 2, stats_pair, (zero, zero))
+    fours = (tile_h - 2) // 4
+    carry = lax.fori_loop(0, fours, stats_four, (zero, zero))
+    if 4 * fours < tile_h - 2:
+        carry = stats_rows(list(range(2 + 4 * fours, tile_h)), carry)
 
     @pl.when(row < n_row - 1)
     def _():

time: 58 us -> 54.9 us (0.947)
  Pallas kernels: 57.8 us -> 54.6 us
    pallas_call x1, Pallas kernels: 30.5 us -> 27.4 us  [body(): pl.pallas_call(functools.partial(front_kernel, n_row, n_col), out_shape=(...]
where the time goes in v3:
time: 54.9 us; the launch traced here: 54.6 us
  Pallas kernels  54.6 us (99%)
    pallas_call x1, Pallas kernels, body(): pl.pallas_call(functools.partial(front_kernel, n_row, n_col), out_shape=(...  27.4 us
    pallas_call x1, Pallas kernels, body(): pl.pallas_call(functools.partial(mid_kernel, n_row, n_col), out_shape=jax...  27.3 us

profile of v3, /device:TPU:0, one launch (start us, length us, event | category | flops | bytes accessed | tf_op | source)
XLA Modules:
  0.0 54.6 jit_solution(12047716000833427621)
XLA Ops:
  0.0 27.4 %shard_map.73 = (bf16[66,80,512]{2,1,0:T(8,128)(2,1)}, f32[8,512]{1,0:T(8,128)}) custom-call(bf16[16,4096]{1,0:T(8,128)(2,1)} %lat_hbm.1, bf16[144,512]{1,0:T(8,128)(2,1)} %bitcast.8, f32[1,512]{1,0:T(1,128)} %bitcast.9, f32[1,512]{1,0:T(1,128)} %bitcast.10, f32[1,512]{1,0:T(1,128)} %bitcast.11), custom_call_target="tpu_custom_call" | custom-call | tf_op jit(solution)/shard_map/pallas_call | solution.py:364
  27.4 27.3 %shard_map.74 = bf16[64,64,512]{2,1,0:T(8,128)(2,1)} custom-call(bf16[66,80,512]{2,1,0:T(8,128)(2,1)} %get-tuple-element.7.fo_hbm, f32[8,512]{1,0:T(8,128)} %get-tuple-element.8.ss_hbm, bf16[9,512,512]{2,1,0:T(8,128)(2,1)} %bitcast.12, f32[1,512]{1,0:T(1,128)} %bitcast.13), custom_call_target="tpu_custom_call" | custom-call | flops 19327352832 | bytes 14680064 | tf_op jit(solution)/shard_map/pallas_call | solution.py:400
